TPU v7x, 32 devices: a whole 2x2x4 slice. The times are simulated.
32 devices in a mesh: mode: 4 (over x, core), batch: 4 (over z), cores: 2 (over y).
Axes of the slice: x: 2, y: 2, z: 4, core: 2. Of those that a mesh axis runs over, the one named last changes fastest.
Arguments:
- fields: bfloat16 [4, 20, 1024, 1024], P('batch', None, ('mode', 'cores')), may hold values from -6 to 6
- lift_weight: bfloat16 [20, 128], replicated, may hold values from -1.25 to 1.25
- lift_bias: float32 [128], replicated, may hold values from -3 to 3
- first_core: bfloat16 [128, 32, 32], P('batch'), may hold values from -1 to 1
- second_core: bfloat16 [128, 32, 32], P(('mode', 'cores')), may hold values from -1 to 1
- input_core: bfloat16 [128, 32, 32], P('batch'), may hold values from -0.09375 to 0.09375
- output_core: bfloat16 [128, 2, 32, 32], P('batch'), may hold values from -3 to 3
- skip_weight: bfloat16 [128, 128], replicated, may hold values from -0.5 to 0.5
- skip_bias: float32 [128], replicated, may hold values from -3 to 3
- out_weight: bfloat16 [128, 20], replicated, may hold values from -0.5 to 0.5
- out_bias: float32 [20], replicated, may hold values from -3 to 3
Outputs:
- updated: bfloat16 [4, 20, 1024, 1024], P('batch', None, ('mode', 'cores'))
All inputs are finite; a program needn't handle non-finite values.
Results may differ from a plain program's by a relative error of at most 0.012.
Values may be sent and summed in bfloat16 or wider, within the bound.
A program may use at most 256 MiB of HBM per device.

v0:
```python
import math
import jax
import jax.numpy as jnp
from jax import lax
from jax.sharding import PartitionSpec as P

NX = 1024
NY = 1024
MX = 128
MY = 128
TWO_PI = 2.0 * math.pi


def wave_pair(waves, points, length):
    phase_step = waves[:, None] * points[None, :] % length
    angles = phase_step.astype(jnp.float32) * (TWO_PI / length)
    return (jnp.cos(angles), jnp.sin(angles))


def width_forward(length, wave_count):
    points = jnp.arange(length, dtype=jnp.int32)
    waves = jnp.arange(wave_count, dtype=jnp.int32)
    cosines, sine_part = wave_pair(points, waves, length)
    stacked = jnp.stack([cosines, -sine_part], axis=1) / math.sqrt(length)
    return stacked.astype(jnp.bfloat16)


def height_forward(row_index, wave_count, length):
    waves = jnp.arange(wave_count, dtype=jnp.int32) - wave_count // 2
    cosines, sine_part = wave_pair(waves, row_index, length)
    upper = jnp.stack([cosines, sine_part], axis=1)
    lower = jnp.stack([-sine_part, cosines], axis=1)
    return (jnp.stack([upper, lower], axis=0) / math.sqrt(length)).astype(jnp.bfloat16)


def height_inverse(row_index, wave_count, length):
    waves = jnp.arange(wave_count, dtype=jnp.int32) - wave_count // 2
    cosines, sine_part = wave_pair(row_index, waves, length)
    upper = jnp.stack([cosines, -sine_part], axis=1)
    lower = jnp.stack([sine_part, cosines], axis=1)
    return (jnp.stack([upper, lower], axis=0) / math.sqrt(length)).astype(jnp.bfloat16)


def width_inverse(waves, length):
    points = jnp.arange(length, dtype=jnp.int32)
    cosines, sine_part = wave_pair(waves, points, length)
    weight = jnp.where(waves == 0, 1.0, 2.0).astype(jnp.float32)[:, None]
    stacked = jnp.stack([cosines * weight, -sine_part * weight], axis=0) / math.sqrt(length)
    return stacked.astype(jnp.bfloat16)


def bias_modes(lift_bias, wave_index, length):
    real_row = (
        jnp.where(wave_index == 0, 1.0, 0.0).astype(jnp.float32)[:, None]
        * (math.sqrt(length) * lift_bias)[None, :]
    )
    return jnp.stack([real_row, jnp.zeros_like(real_row)], axis=0)


def lift_modes(modes, lift_weight, lift_bias, wave_index):
    lifted_modes = jnp.einsum(
        "fabpmv,vc->fabpmc", modes, lift_weight, preferred_element_type=jnp.float32
    )
    return (lifted_modes + bias_modes(lift_bias, wave_index, NY)).astype(jnp.bfloat16)


def grid_rows(stored, row_count, holder_count):
    return stored % row_count * holder_count + stored // row_count


def shards(
    fields,
    lift_weight,
    lift_bias,
    first_core,
    second_core,
    input_core,
    output_core,
    skip_weight,
    skip_bias,
    out_weight,
    out_bias,
):
    mode_count = lax.axis_size("mode")
    core_count = lax.axis_size("cores")
    row_count = fields.shape[2]
    block_size = second_core.shape[0]
    block_start = (lax.axis_index("mode") * core_count + lax.axis_index("cores")) * block_size
    local_waves = block_start + jnp.arange(block_size, dtype=jnp.int32)
    lifted = (
        jnp.einsum("fvxy,vc->fxyc", fields, lift_weight, preferred_element_type=jnp.float32)
        + lift_bias
    ).astype(jnp.bfloat16)
    field_modes = jnp.einsum(
        "fvxy,ypk->fxpkv", fields, width_forward(NY, MY), preferred_element_type=jnp.float32
    ).astype(jnp.bfloat16)
    field_modes = field_modes[:, None]
    gathered = (
        lax.all_gather(first_core, "batch", axis=0, tiled=True),
        lax.all_gather(input_core, "batch", axis=0, tiled=True),
        lax.all_gather(output_core, "batch", axis=0, tiled=True),
    )
    first_whole, input_whole, output_whole = gathered
    mode_factor = jnp.einsum(
        "kab,mbd->kmad", first_whole, second_core, preferred_element_type=jnp.float32
    ).astype(jnp.bfloat16)
    arrived = lax.all_to_all(
        field_modes, ("mode", "cores"), split_axis=4, concat_axis=2, tiled=True
    )
    rows_held = jnp.arange(NX, dtype=jnp.int32)[None, :]
    by_mode = lift_modes(arrived, lift_weight, lift_bias, local_waves)
    lead_rows = rows_held.shape[0]
    side_rows = rows_held.shape[1]
    flat_rows = grid_rows(rows_held.reshape(-1), row_count, mode_count * core_count)
    height_table = height_forward(flat_rows, MX, NX).reshape(2, MX, 2, lead_rows, side_rows)
    spectrum = jnp.einsum(
        "qkpab,fabpmc->fqkmc", height_table, by_mode, preferred_element_type=jnp.float32
    ).astype(jnp.bfloat16)
    projected = jnp.einsum(
        "fqkmc,cbe->fqkmbe", spectrum, input_whole, preferred_element_type=jnp.float32
    ).astype(jnp.bfloat16)
    carried = jnp.einsum(
        "kmab,fqkmbe->fqkmae", mode_factor, projected, preferred_element_type=jnp.float32
    ).astype(jnp.bfloat16)
    traced = jnp.einsum(
        "fqkmae,osea->fqkmso", carried, output_whole, preferred_element_type=jnp.float32
    )
    real_part = traced[:, 0, :, :, 0, :] - traced[:, 1, :, :, 1, :]
    imaginary = traced[:, 0, :, :, 1, :] + traced[:, 1, :, :, 0, :]
    mixed_modes = jnp.stack([real_part, imaginary], axis=1).astype(jnp.bfloat16)
    height_back = height_inverse(flat_rows, MX, NX).reshape(2, lead_rows, side_rows, 2, MX)
    col_modes = jnp.einsum(
        "pabqk,fqkmc->fabpmc", height_back, mixed_modes, preferred_element_type=jnp.float32
    ).astype(jnp.bfloat16)
    returned = lax.all_to_all(col_modes, ("mode", "cores"), split_axis=2, concat_axis=4, tiled=True)
    waves_held = jnp.arange(MY, dtype=jnp.int32)
    width_back = width_inverse(waves_held, NY)
    spatial = jnp.einsum(
        "fxpmc,pmy->fxyc", returned[:, 0], width_back, preferred_element_type=jnp.float32
    )
    skip_term = jnp.einsum("fxyc,cd->fxyd", lifted, skip_weight, preferred_element_type=jnp.float32)
    active = jax.nn.gelu(spatial + skip_term + skip_bias, approximate=False).astype(jnp.bfloat16)
    result = (
        jnp.einsum("fxyc,cv->fvxy", active, out_weight, preferred_element_type=jnp.float32)
        + out_bias[:, None, None]
    )
    return result.astype(jnp.bfloat16)


def solution(mesh):
    placed = (
        P("batch", None, ("mode", "cores"), None),
        P(),
        P(),
        P("batch", None, None),
        P(("mode", "cores"), None, None),
        P("batch", None, None),
        P("batch", None, None, None),
        P(),
        P(),
        P(),
        P(),
    )
    return jax.shard_map(
        shards,
        mesh=mesh,
        in_specs=placed,
        out_specs=P("batch", None, ("mode", "cores"), None),
        check_vma=False,
    )
```

profile of v0, /device:TPU:0, one launch (start us, length us, event | category | flops | bytes accessed | tf_op | source)
XLA Modules:
  0.0 632.1 jit_solution(4444873286141601486)
XLA Ops:
  0.0 2.1 sine_negate_fusion
  2.1 4.1 fusion.36
  6.1 2.4 copy.49
  8.6 5.2 all-to-all-start
  14.4 1.8 copy.59
  16.3 22.9 %all_gather.10 = bf16[128,32,32]{2,1,0:T(8,128)(2,1)S(1)} all-gather(bf16[32,32,32]{2,1,0:T(8,128)(2,1)} %param.14), channel_id=1, replica_groups=mesh['mode'=4,'batch'=4,'cores'=2] {'batch'}, dimensions={0}, use_global_device_ids=true | all-gather | bytes 327680 | tf_op jit(solution)/shard_map/all_gather | solution.py:99
  39.2 3.3 convert_bitcast_fusion.1
  42.5 23.0 %copy.75 = bf16[128,16,32,32,1]{3,2,4,1,0:T(8,128)(2,1)} copy(bf16[128,16,32,32,1]{0,3,2,1,4:T(8,128)(2,1)} %convert_bitcast_fusion.1) | data formatting | bytes 8388608 | tf_op jit(solution)/shard_map/convert_element_type | solution.py:106
  65.6 24.2 %all_gather.9 = bf16[128,32,32]{2,1,0:T(8,128)(2,1)} all-gather(bf16[32,32,32]{2,1,0:T(8,128)(2,1)} %param.16), channel_id=1, replica_groups=mesh['mode'=4,'batch'=4,'cores'=2] {'batch'}, dimensions={0}, use_global_device_ids=true | all-gather | bytes 327680 | tf_op jit(solution)/shard_map/all_gather | solution.py:100
  89.8 2.1 fusion.87
  92.0 1.6 maximum_bitcast_fusion
  93.5 2.1 fusion.92
  95.6 1.6 maximum_bitcast_fusion.3
  97.2 36.8 %all_gather.11 = bf16[128,2,32,32]{2,0,3,1:T(8,128)(2,1)} all-gather(bf16[32,2,32,32]{2,0,3,1:T(8,128)(2,1)S(1)} %copy.59), channel_id=1, replica_groups=mesh['mode'=4,'batch'=4,'cores'=2] {'batch'}, dimensions={0}, use_global_device_ids=true | all-gather | bytes 655360 | tf_op jit(solution)/shard_map/all_gather | solution.py:101
  134.1 0.8 copy.118
  134.9 0.9 reshape.755
  135.8 8.7 %fusion.39 = bf16[2,128,16,128,1]{1,3,0,2,4:T(8,128)(2,1)S(1)} fusion(f32[2,16,128]{2,0,1:T(2,128)S(1)} %stack.59, bf16[1024,2,16,20]{0,2,3,1:T(8,128)(2,1)S(1)} %reshape.755, f32[1,128,2,1024]{3,1,2,0:T(8,128)} %get-tuple-element.6, f32[1,128,2,1024]{3,1,2,0:T(8,128)} %get-tuple-element.5, bf16[20,128]{1,0:T(8,128)(2,1)} %param.12), kind=kOutput, calls=%fused_computation.50 | convolution fusion | flops 2325741568 | bytes 4477952 | tf_op jit(solution)/shard_map/qkpab,fabpmc->fqkmc/dot_general | solution.py:116
  144.5 6.9 %convolution_convert_fusion = bf16[2,128,16,32,32]{1,4,3,2,0:T(8,128)(2,1)} fusion(bf16[128,32,32,1,1]{2,1,0,4,3:T(8,128)(2,1)} %bitcast.201, bf16[2,128,16,128,1]{1,3,0,2,4:T(8,128)(2,1)S(1)} %fusion.39), kind=kOutput, calls=%fused_computation.36 | convolution fusion | flops 1077936128 | bytes 9699328 | tf_op jit(solution)/shard_map/fqkmc,cbe->fqkmbe/dot_general | solution.py:119
  151.4 54.9 %copy.57 = bf16[2,128,16,32,32]{3,4,0,2,1:T(8,128)(2,1)} copy(bf16[2,128,16,32,32]{1,4,3,2,0:T(8,128)(2,1)} %convolution_convert_fusion) | data formatting | bytes 16777216 | tf_op jit(solution)/shard_map/convert_element_type | solution.py:121
  206.3 28.3 %convert_bitcast_fusion = bf16[2,128,16,32,32,1]{3,4,0,2,1,5:T(8,128)(2,1)} fusion(bf16[2,128,16,32,32]{3,4,0,2,1:T(8,128)(2,1)} %copy.57, bf16[128,16,32,32,1]{3,2,4,1,0:T(8,128)(2,1)} %copy.75), kind=kOutput, calls=%fused_computation.26 | convolution fusion | flops 272629760 | bytes 20971520 | tf_op jit(solution)/shard_map/kmab,fqkmbe->fqkmae/dot_general | solution.py:122
  234.6 47.5 %copy.76 = bf16[2,128,16,32,32,1]{1,4,3,5,2,0:T(8,128)(2,1)} copy(bf16[2,128,16,32,32,1]{3,4,0,2,1,5:T(8,128)(2,1)} %convert_bitcast_fusion) | data formatting | bytes 16777216 | tf_op jit(solution)/shard_map/reshape.14
  282.1 12.4 %convolution_bitcast_fusion = f32[1,2,128,16,2,128]{5,2,4,3,1,0:T(8,128)S(1)} fusion(bf16[2,128,16,32,32,1]{1,4,3,5,2,0:T(8,128)(2,1)} %copy.76, bf16[128,2,32,32]{2,0,3,1:T(8,128)(2,1)} %all_gather.11), kind=kOutput, calls=%fused_computation.40 | convolution fusion | flops 2147483648 | bytes 13107200 | tf_op jit(solution)/shard_map/fqkmae,osea->fqkmso/dot_general | solution.py:125
  294.8 5.6 fusion.21
  300.4 21.3 %copy.65 = bf16[1,1,1024,2,16,128]{5,3,4,1,0,2:T(2,128)(2,1)} copy(bf16[1,1,1024,2,16,128]{2,5,3,4,1,0:T(8,128)(2,1)} %fusion.21) | data formatting | bytes 16777216 | tf_op jit(solution)/shard_map/convert_element_type | solution.py:134
  321.7 5.1 all-to-all-start.1
  326.8 2.1 cosine_multiply_fusion
  328.9 27.3 %fusion.19 = f32[128,1024,128]{2,1,0:T(8,128)} fusion(bf16[20,128,1024]{2,1,0:T(8,128)(2,1)} %bitcast.198, bf16[20,128]{1,0:T(8,128)(2,1)S(1)} %copy-done.4), kind=kOutput, calls=%fused_computation.33 | convolution fusion | flops 671088640 | bytes 72356864 | tf_op jit(solution)/shard_map/fvxy,vc->fxyc/dot_general | solution.py:91
  356.2 63.7 %all-to-all-done.1 = bf16[1,1,1024,2,16,128]{5,3,4,1,0,2:T(2,128)(2,1)} async-done(((bf16[1,1,1024,2,16,128]{5,3,4,1,0,2:T(2,128)(2,1)}), bf16[1,1,1024,2,16,128]{5,3,4,1,0,2:T(2,128)(2,1)}, u32[]{:S(2)}, u32[]{:S(2)}) %all-to-all-start.1) | async-done | bytes 8388640 | tf_op jit(solution)/shard_map/all_to_all | solution.py:135
  420.0 9.1 %copy.66 = bf16[1,1,8,128,2,16,128]{6,5,2,4,3,1,0:T(8,128)(2,1)} copy(bf16[1,1,8,128,2,16,128]{6,4,5,3,2,1,0:T(2,128)(2,1)} %bitcast.50) | data formatting | bytes 16777216 | tf_op jit(solution)/shard_map/all_to_all | solution.py:135
  429.1 26.7 %fusion.75 = f32[1024,128,128,1]{2,0,3,1:T(8,128)} fusion(bf16[128,2,128,128]{3,2,1,0:T(8,128)(2,1)} %bitcast.197, f32[1,128,1024]{1,2,0:T(8,128)S(1)} %get-tuple-element.16, f32[1,128,1024]{1,2,0:T(8,128)S(1)} %get-tuple-element.15), kind=kOutput, calls=%fused_computation.106 | convolution fusion | flops 8590721024 | bytes 76546048 | tf_op jit(solution)/shard_map/fxpmc,pmy->fxyc/dot_general | solution.py:138
  455.8 167.8 %fusion.18 = bf16[1,20,128,1024]{3,1,2,0:T(8,128)(2,1)} fusion(f32[20]{0:T(128)S(1)} %copy-done.7, f32[128]{0:T(128)S(1)} %copy-done.8, f32[1024,128,128,1]{2,0,3,1:T(8,128)} %fusion.75, f32[128,1024,128]{2,1,0:T(8,128)} %fusion.19, f32[128]{0:T(128)S(1)} %copy-done.9, bf16[128,128]{1,0:T(8,128)(2,1)S(1)} %copy-done.5, bf16[128,20]{0,1:T(8,128)(2,1)S(1)} %copy-done.6), kind=kOutput, calls=%fused_computation.32 | convolution fusion | flops 6128926720 | bytes 139499600 | tf_op jit(solution)/shard_map/fxyc,cv->fvxy/dot_general | solution.py:144
  623.6 8.1 %copy.68 = bf16[1,20,128,1024]{3,2,1,0:T(8,128)(2,1)} copy(bf16[1,20,128,1024]{3,1,2,0:T(8,128)(2,1)} %fusion.18) | data formatting | bytes 10485760 | tf_op jit(solution)/shard_map/convert_element_type | solution.py:147
  (30 shorter events, 1.0 us)
Async XLA Ops:
  0.0 39.2 %copy-start = (bf16[16,32,32]{2,1,0:T(8,128)(2,1)S(1)}, bf16[16,32,32]{2,1,0:T(8,128)(2,1)}, u32[]{:S(2)}) copy-start(bf16[16,32,32]{2,1,0:T(8,128)(2,1)} %param.15) | copy-start | bytes 98308
  8.6 125.5 %all-to-all-start = ((bf16[1,1,128,2,128,20]{2,3,5,1,0,4:T(2,128)(2,1)}), bf16[1,1,128,2,128,20]{2,3,5,1,0,4:T(2,128)(2,1)S(1)}, u32[]{:S(2)}, u32[]{:S(2)}) async-start(bf16[1,1,128,2,128,20]{2,3,5,1,0,4:T(2,128)(2,1)} %copy.49), calls=%async_computation | async-start | bytes 2621440 | tf_op jit(solution)/shard_map/all_to_all | solution.py:107
  234.6 60.2 %copy-start.2 = (f32[1,1024,2,128]{1,3,2,0:T(8,128)S(1)}, f32[1,1024,2,128]{1,3,2,0:T(8,128)}, u32[]{:S(2)}) copy-start(f32[1,1024,2,128]{1,3,2,0:T(8,128)} %get-tuple-element.7) | copy-start | bytes 3145732
  234.6 60.2 %copy-start.3 = (f32[1,1024,2,128]{1,3,2,0:T(8,128)S(1)}, f32[1,1024,2,128]{1,3,2,0:T(8,128)}, u32[]{:S(2)}) copy-start(f32[1,1024,2,128]{1,3,2,0:T(8,128)} %get-tuple-element.8) | copy-start | bytes 3145732
  234.6 94.3 %copy-start.4 = (bf16[20,128]{1,0:T(8,128)(2,1)S(1)}, bf16[20,128]{1,0:T(8,128)(2,1)}, u32[]{:S(2)}) copy-start(bf16[20,128]{1,0:T(8,128)(2,1)} %param.12) | copy-start | bytes 15364
  321.7 98.3 %all-to-all-start.1 = ((bf16[1,1,1024,2,16,128]{5,3,4,1,0,2:T(2,128)(2,1)}), bf16[1,1,1024,2,16,128]{5,3,4,1,0,2:T(2,128)(2,1)}, u32[]{:S(2)}, u32[]{:S(2)}) async-start(bf16[1,1,1024,2,16,128]{5,3,4,1,0,2:T(2,128)(2,1)} %copy.65), calls=%async_computation.1 | async-start | bytes 16777216 | tf_op jit(solution)/shard_map/all_to_all | solution.py:135
  356.2 99.6 %copy-start.5 = (bf16[128,128]{1,0:T(8,128)(2,1)S(1)}, bf16[128,128]{1,0:T(8,128)(2,1)}, u32[]{:S(2)}) copy-start(bf16[128,128]{1,0:T(8,128)(2,1)} %param.18) | copy-start | bytes 98308
  356.2 99.6 %copy-start.6 = (bf16[128,20]{0,1:T(8,128)(2,1)S(1)}, bf16[128,20]{0,1:T(8,128)(2,1)}, u32[]{:S(2)}) copy-start(bf16[128,20]{0,1:T(8,128)(2,1)} %param.20) | copy-start | bytes 15364
  356.2 99.6 %copy-start.7 = (f32[20]{0:T(128)S(1)}, f32[20]{0:T(128)}, u32[]{:S(2)}) copy-start(f32[20]{0:T(128)} %param.21) | copy-start | bytes 244
  356.2 99.6 %copy-start.8 = (f32[128]{0:T(128)S(1)}, f32[128]{0:T(128)}, u32[]{:S(2)}) copy-start(f32[128]{0:T(128)} %param.19) | copy-start | bytes 1540
  356.2 99.6 %copy-start.9 = (f32[128]{0:T(128)S(1)}, f32[128]{0:T(128)}, u32[]{:S(2)}) copy-start(f32[128]{0:T(128)} %param.13) | copy-start | bytes 1540
  455.8 175.9 %copy-start.1 = (bf16[16,32,32]{2,1,0:T(8,128)(2,1)S(1)}, bf16[16,32,32]{2,1,0:T(8,128)(2,1)}, u32[]{:S(2)}) copy-start(bf16[16,32,32]{2,1,0:T(8,128)(2,1)} %param.15) | copy-start | bytes 98308
where the time goes:
time: 640 us; the launch traced here: 632 us
  matrix products  291 us (45%)
  local copies, waits for them, and re-layouts  170 us (27%)
  blocking collectives  83.9 us (13%)
  waiting for transfers between devices  63.8 us (10%)
  other arithmetic  12.5 us (2%)
  starting transfers between devices  10.3 us (2%)
    dot_general x1, matrix products, shards(): jnp.einsum('fxyc,cv->fvxy', active, out_weight, preferred_element_type=jn...  168 us
    all_to_all x1, waiting for transfers between devices, shards(): lax.all_to_all(col_modes, ('mode', 'cores'), split_axis=2, concat_axis=4,...  63.7 us
    convert_element_type x1, local copies, waits for them, and re-layouts, shards(): projected = jnp.einsum('fqkmc,cbe->fqkmbe', spectrum, input_whole, prefer...  54.9 us
    another operation x2, local copies, waits for them, and re-layouts  48.3 us
    all_gather x1, blocking collectives, shards(): lax.all_gather(output_core, 'batch', axis=0, tiled=True)  36.8 us
    dot_general x1, matrix products, shards(): jnp.einsum('kmab,fqkmbe->fqkmae', mode_factor, projected, preferred_eleme...  28.3 us
    dot_general x1, matrix products, shards(): jnp.einsum('fvxy,vc->fxyc', fields, lift_weight, preferred_element_type=j...  27.3 us
    dot_general x1, matrix products, shards(): jnp.einsum('fxpmc,pmy->fxyc', returned[:, 0], width_back, preferred_eleme...  26.7 us
  transfers between devices with their start and end apart: 2, of which 1 were waited for; matrix products, arithmetic and copies ran while one was open for 10% of the time, Pallas kernels for 0%

commit v1 on v0

--- a/solution.py
+++ b/solution.py
@@ -132,7 +132,15 @@
     col_modes = jnp.einsum(
         "pabqk,fqkmc->fabpmc", height_back, mixed_modes, preferred_element_type=jnp.float32
     ).astype(jnp.bfloat16)
-    returned = lax.all_to_all(col_modes, ("mode", "cores"), split_axis=2, concat_axis=4, tiled=True)
+    returned = jnp.concatenate(
+        lax.all_to_all(
+            jnp.stack(jnp.split(col_modes, lax.axis_size(("mode", "cores")), axis=2)),
+            ("mode", "cores"),
+            0,
+            0,
+        ),
+        axis=4,
+    )
     waves_held = jnp.arange(MY, dtype=jnp.int32)
     width_back = width_inverse(waves_held, NY)
     spatial = jnp.einsum(

time: 640 us -> 625 us (0.977)
  local copies, waits for them, and re-layouts: 170 us -> 162 us
    convert_element_type x1 -> x0, local copies, waits for them, and re-layouts: 21.3 us -> none  [shards(): col_modes = jnp.einsum('pabqk,fqkmc->fabpmc', height_back, mixed_modes, p...]
    another operation x2 -> x4, local copies, waits for them, and re-layouts: 48.3 us -> 62 us
    all_to_all x1 -> x0, local copies, waits for them, and re-layouts: 9.14 us -> none  [shards(): lax.all_to_all(col_modes, ('mode', 'cores'), split_axis=2, concat_axis=4,...]
    unnamed x21 -> x32, local copies, waits for them, and re-layouts: 1.87 us -> 10.9 us
  transfers between devices with their start and end apart: 2 -> 2, of which waited for: 1 -> 1; matrix products, arithmetic and copies ran while one was open for 10% -> 11% of each run, Pallas kernels for 0% -> 0%
where the time goes in v1:
time: 625 us; the launch traced here: 618 us
  matrix products  287 us (46%)
  local copies, waits for them, and re-layouts  162 us (26%)
  blocking collectives  81.4 us (13%)
  waiting for transfers between devices  63.8 us (10%)
  other arithmetic  12.5 us (2%)
  starting transfers between devices  10.3 us (2%)
    dot_general x1, matrix products, shards(): jnp.einsum('fxyc,cv->fvxy', active, out_weight, preferred_element_type=jn...  168 us
    all_to_all x1, waiting for transfers between devices, shards(): lax.all_to_all(jnp.stack(jnp.split(col_modes, lax.axis_size(('mode', 'cor...  63.8 us
    another operation x3, local copies, waits for them, and re-layouts  60.7 us
    convert_element_type x1, local copies, waits for them, and re-layouts, shards(): projected = jnp.einsum('fqkmc,cbe->fqkmbe', spectrum, input_whole, prefer...  54.9 us
    all_gather x1, blocking collectives, shards(): lax.all_gather(output_core, 'batch', axis=0, tiled=True)  35.4 us
    dot_general x1, matrix products, shards(): jnp.einsum('kmab,fqkmbe->fqkmae', mode_factor, projected, preferred_eleme...  28.2 us
    dot_general x1, matrix products, shards(): jnp.einsum('fvxy,vc->fxyc', fields, lift_weight, preferred_element_type=j...  27.3 us
    dot_general x1, matrix products, shards(): jnp.einsum('fxpmc,pmy->fxyc', returned[:, 0], width_back, preferred_eleme...  26.6 us
  transfers between devices with their start and end apart: 2, of which 1 were waited for; matrix products, arithmetic and copies ran while one was open for 11% of the time, Pallas kernels for 0%

profile of v1, /device:TPU:0, one launch (start us, length us, event | category | flops | bytes accessed | tf_op | source)
XLA Modules:
  0.0 618.0 jit_solution(10670639023242473408)
XLA Ops:
  0.0 2.1 sine_negate_fusion
  2.1 4.1 fusion.36
  6.1 2.4 copy.48
  8.6 5.2 all-to-all-start
  14.4 1.8 copy.58
  16.3 22.9 %all_gather.10 = bf16[128,32,32]{2,1,0:T(8,128)(2,1)S(1)} all-gather(bf16[32,32,32]{2,1,0:T(8,128)(2,1)} %param.14), channel_id=1, replica_groups=mesh['mode'=4,'batch'=4,'cores'=2] {'batch'}, dimensions={0}, use_global_device_ids=true | all-gather | bytes 327680 | tf_op jit(solution)/shard_map/all_gather | solution.py:99
  39.2 3.3 convert_bitcast_fusion.1
  42.5 23.1 %copy.73 = bf16[128,16,32,32,1]{3,2,4,1,0:T(8,128)(2,1)} copy(bf16[128,16,32,32,1]{0,3,2,1,4:T(8,128)(2,1)} %convert_bitcast_fusion.1) | data formatting | bytes 8388608 | tf_op jit(solution)/shard_map/convert_element_type | solution.py:106
  65.6 23.1 %all_gather.9 = bf16[128,32,32]{2,1,0:T(8,128)(2,1)} all-gather(bf16[32,32,32]{2,1,0:T(8,128)(2,1)S(1)} %copy-done.5), channel_id=1, replica_groups=mesh['mode'=4,'batch'=4,'cores'=2] {'batch'}, dimensions={0}, use_global_device_ids=true | all-gather | bytes 327680 | tf_op jit(solution)/shard_map/all_gather | solution.py:100
  88.8 2.1 fusion.95
  90.9 1.6 maximum_bitcast_fusion
  92.4 2.1 fusion.100
  94.6 1.6 maximum_bitcast_fusion.3
  96.1 35.4 %all_gather.11 = bf16[128,2,32,32]{2,0,3,1:T(8,128)(2,1)} all-gather(bf16[32,2,32,32]{2,0,3,1:T(8,128)(2,1)S(1)} %copy.58), channel_id=1, replica_groups=mesh['mode'=4,'batch'=4,'cores'=2] {'batch'}, dimensions={0}, use_global_device_ids=true | all-gather | bytes 655360 | tf_op jit(solution)/shard_map/all_gather | solution.py:101
  133.2 8.7 %fusion.39 = bf16[2,128,16,128,1]{1,3,0,2,4:T(8,128)(2,1)S(1)} fusion(f32[2,16,128]{2,0,1:T(2,128)S(1)} %stack.86, bf16[1024,2,16,20]{0,2,3,1:T(8,128)(2,1)S(1)} %reshape.757, f32[1,128,2,1024]{3,1,2,0:T(8,128)} %get-tuple-element.6, f32[1,128,2,1024]{3,1,2,0:T(8,128)} %get-tuple-element.5, bf16[20,128]{1,0:T(8,128)(2,1)S(1)} %copy-done.6), kind=kOutput, calls=%fused_computation.50 | convolution fusion | flops 2325741568 | bytes 4477952 | tf_op jit(solution)/shard_map/qkpab,fabpmc->fqkmc/dot_general | solution.py:116
  141.9 6.9 %convolution_convert_fusion = bf16[2,128,16,32,32]{1,4,3,2,0:T(8,128)(2,1)} fusion(bf16[128,32,32,1,1]{2,1,0,4,3:T(8,128)(2,1)} %bitcast.231, bf16[2,128,16,128,1]{1,3,0,2,4:T(8,128)(2,1)S(1)} %fusion.39), kind=kOutput, calls=%fused_computation.36 | convolution fusion | flops 1077936128 | bytes 9699328 | tf_op jit(solution)/shard_map/fqkmc,cbe->fqkmbe/dot_general | solution.py:119
  148.9 54.9 %copy.56 = bf16[2,128,16,32,32]{3,4,0,2,1:T(8,128)(2,1)} copy(bf16[2,128,16,32,32]{1,4,3,2,0:T(8,128)(2,1)} %convolution_convert_fusion) | data formatting | bytes 16777216 | tf_op jit(solution)/shard_map/convert_element_type | solution.py:121
  203.8 28.2 %convert_bitcast_fusion = bf16[2,128,16,32,32,1]{3,4,0,2,1,5:T(8,128)(2,1)} fusion(bf16[2,128,16,32,32]{3,4,0,2,1:T(8,128)(2,1)} %copy.56, bf16[128,16,32,32,1]{3,2,4,1,0:T(8,128)(2,1)} %copy.73), kind=kOutput, calls=%fused_computation.26 | convolution fusion | flops 272629760 | bytes 20971520 | tf_op jit(solution)/shard_map/kmab,fqkmbe->fqkmae/dot_general | solution.py:122
  232.0 47.5 %copy.74 = bf16[2,128,16,32,32,1]{1,4,3,5,2,0:T(8,128)(2,1)} copy(bf16[2,128,16,32,32,1]{3,4,0,2,1,5:T(8,128)(2,1)} %convert_bitcast_fusion) | data formatting | bytes 16777216 | tf_op jit(solution)/shard_map/reshape.15
  279.5 11.9 %convolution_bitcast_fusion = f32[1,2,128,16,2,128]{5,2,4,3,1,0:T(8,128)S(1)} fusion(bf16[2,128,16,32,32,1]{1,4,3,5,2,0:T(8,128)(2,1)} %copy.74, bf16[128,2,32,32]{2,0,3,1:T(8,128)(2,1)S(1)} %copy-done.4), kind=kOutput, calls=%fused_computation.40 | convolution fusion | flops 2147483648 | bytes 13107200 | tf_op jit(solution)/shard_map/fqkmae,osea->fqkmso/dot_general | solution.py:125
  291.7 2.4 fusion.21
  294.0 1.3 fusion.55
  299.2 1.3 fusion.51
  303.0 1.3 fusion.48
  304.3 5.1 all-to-all-start.1
  309.5 2.1 cosine_multiply_fusion
  311.6 27.3 %fusion.19 = f32[128,1024,128]{2,1,0:T(8,128)} fusion(bf16[20,128,1024]{2,1,0:T(8,128)(2,1)} %bitcast.228, bf16[20,128]{1,0:T(8,128)(2,1)S(1)} %copy-done.6), kind=kOutput, calls=%fused_computation.33 | convolution fusion | flops 671088640 | bytes 72356864 | tf_op jit(solution)/shard_map/fvxy,vc->fxyc/dot_general | solution.py:91
  338.9 63.8 %all-to-all-done.1 = bf16[8,1,1,128,2,16,128]{3,6,4,5,2,1,0:T(8,128)(2,1)} async-done(((bf16[8,1,1,128,2,16,128]{3,6,4,5,2,1,0:T(8,128)(2,1)}), bf16[8,1,1,128,2,16,128]{3,6,4,5,2,1,0:T(8,128)(2,1)}, u32[]{:S(2)}, u32[]{:S(2)}) %all-to-all-start.1) | async-done | bytes 8388640 | tf_op jit(solution)/shard_map/all_to_all | solution.py:136
  402.6 12.4 %copy.64 = bf16[128,2,128,128]{3,2,1,0:T(8,128)(2,1)} copy(bf16[128,2,128,128]{0,3,1,2:T(8,128)(2,1)} %bitcast.60) | data formatting | bytes 16777216 | tf_op jit(solution)/shard_map/reshape.20
  415.1 26.6 %fusion.83 = f32[1024,128,128,1]{2,0,3,1:T(8,128)} fusion(bf16[128,2,128,128]{3,2,1,0:T(8,128)(2,1)} %copy.64, f32[1,128,1024]{1,2,0:T(8,128)S(1)} %get-tuple-element.16, f32[1,128,1024]{1,2,0:T(8,128)S(1)} %get-tuple-element.15), kind=kOutput, calls=%fused_computation.122 | convolution fusion | flops 8590721024 | bytes 76546048 | tf_op jit(solution)/shard_map/fxpmc,pmy->fxyc/dot_general | solution.py:146
  441.7 167.8 %fusion.18 = bf16[1,20,128,1024]{3,1,2,0:T(8,128)(2,1)} fusion(f32[20]{0:T(128)S(1)} %copy-done.9, f32[128]{0:T(128)S(1)} %copy-done.10, f32[1024,128,128,1]{2,0,3,1:T(8,128)} %fusion.83, f32[128,1024,128]{2,1,0:T(8,128)} %fusion.19, f32[128]{0:T(128)S(1)} %copy-done.11, bf16[128,128]{1,0:T(8,128)(2,1)S(1)} %copy-done.7, bf16[128,20]{0,1:T(8,128)(2,1)S(1)} %copy-done.8), kind=kOutput, calls=%fused_computation.32 | convolution fusion | flops 6128926720 | bytes 139499600 | tf_op jit(solution)/shard_map/fxyc,cv->fvxy/dot_general | solution.py:152
  609.5 8.1 %copy.66 = bf16[1,20,128,1024]{3,2,1,0:T(8,128)(2,1)} copy(bf16[1,20,128,1024]{3,1,2,0:T(8,128)(2,1)} %fusion.18) | data formatting | bytes 10485760 | tf_op jit(solution)/shard_map/convert_element_type | solution.py:155
  (41 shorter events, 9.0 us)
Async XLA Ops:
  0.0 39.2 %copy-start = (bf16[16,32,32]{2,1,0:T(8,128)(2,1)S(1)}, bf16[16,32,32]{2,1,0:T(8,128)(2,1)}, u32[]{:S(2)}) copy-start(bf16[16,32,32]{2,1,0:T(8,128)(2,1)} %param.15) | copy-start | bytes 98308
  0.0 65.6 %copy-start.5 = (bf16[32,32,32]{2,1,0:T(8,128)(2,1)S(1)}, bf16[32,32,32]{2,1,0:T(8,128)(2,1)}, u32[]{:S(2)}) copy-start(bf16[32,32,32]{2,1,0:T(8,128)(2,1)} %param.16) | copy-start | bytes 196612
  0.0 133.2 %copy-start.6 = (bf16[20,128]{1,0:T(8,128)(2,1)S(1)}, bf16[20,128]{1,0:T(8,128)(2,1)}, u32[]{:S(2)}) copy-start(bf16[20,128]{1,0:T(8,128)(2,1)} %param.12) | copy-start | bytes 15364
  8.6 123.0 %all-to-all-start = ((bf16[1,1,128,2,128,20]{2,3,5,1,0,4:T(2,128)(2,1)}), bf16[1,1,128,2,128,20]{2,3,5,1,0,4:T(2,128)(2,1)S(1)}, u32[]{:S(2)}, u32[]{:S(2)}) async-start(bf16[1,1,128,2,128,20]{2,3,5,1,0,4:T(2,128)(2,1)} %copy.48), calls=%async_computation | async-start | bytes 2621440 | tf_op jit(solution)/shard_map/all_to_all | solution.py:107
  232.0 47.5 %copy-start.4 = (bf16[128,2,32,32]{2,0,3,1:T(8,128)(2,1)S(1)}, bf16[128,2,32,32]{2,0,3,1:T(8,128)(2,1)}, u32[]{:S(2)}) copy-start(bf16[128,2,32,32]{2,0,3,1:T(8,128)(2,1)} %all_gather.11) | copy-start | bytes 1572868
  279.5 12.2 %copy-start.2 = (f32[1,1024,2,128]{1,3,2,0:T(8,128)S(1)}, f32[1,1024,2,128]{1,3,2,0:T(8,128)}, u32[]{:S(2)}) copy-start(f32[1,1024,2,128]{1,3,2,0:T(8,128)} %get-tuple-element.7) | copy-start | bytes 3145732
  279.5 12.2 %copy-start.3 = (f32[1,1024,2,128]{1,3,2,0:T(8,128)S(1)}, f32[1,1024,2,128]{1,3,2,0:T(8,128)}, u32[]{:S(2)}) copy-start(f32[1,1024,2,128]{1,3,2,0:T(8,128)} %get-tuple-element.8) | copy-start | bytes 3145732
  304.3 98.3 %all-to-all-start.1 = ((bf16[8,1,1,128,2,16,128]{3,6,4,5,2,1,0:T(8,128)(2,1)}), bf16[8,1,1,128,2,16,128]{3,6,4,5,2,1,0:T(8,128)(2,1)}, u32[]{:S(2)}, u32[]{:S(2)}) async-start(bf16[8,1,1,128,2,16,128]{3,6,4,5,2,1,0:T(8,128)(2,1)} %fusion.48), calls=%async_computation.1 | async-start | bytes 16777216 | tf_op jit(solution)/shard_map/all_to_all | solution.py:136
  415.0 26.6 %copy-start.7 = (bf16[128,128]{1,0:T(8,128)(2,1)S(1)}, bf16[128,128]{1,0:T(8,128)(2,1)}, u32[]{:S(2)}) copy-start(bf16[128,128]{1,0:T(8,128)(2,1)} %param.18) | copy-start | bytes 98308
  415.0 26.6 %copy-start.8 = (bf16[128,20]{0,1:T(8,128)(2,1)S(1)}, bf16[128,20]{0,1:T(8,128)(2,1)}, u32[]{:S(2)}) copy-start(bf16[128,20]{0,1:T(8,128)(2,1)} %param.20) | copy-start | bytes 15364
  415.0 26.6 %copy-start.9 = (f32[20]{0:T(128)S(1)}, f32[20]{0:T(128)}, u32[]{:S(2)}) copy-start(f32[20]{0:T(128)} %param.21) | copy-start | bytes 244
  415.0 26.6 %copy-start.10 = (f32[128]{0:T(128)S(1)}, f32[128]{0:T(128)}, u32[]{:S(2)}) copy-start(f32[128]{0:T(128)} %param.19) | copy-start | bytes 1540
  415.1 26.6 %copy-start.11 = (f32[128]{0:T(128)S(1)}, f32[128]{0:T(128)}, u32[]{:S(2)}) copy-start(f32[128]{0:T(128)} %param.13) | copy-start | bytes 1540
  441.7 175.9 %copy-start.1 = (bf16[16,32,32]{2,1,0:T(8,128)(2,1)S(1)}, bf16[16,32,32]{2,1,0:T(8,128)(2,1)}, u32[]{:S(2)}) copy-start(bf16[16,32,32]{2,1,0:T(8,128)(2,1)} %param.15) | copy-start | bytes 98308
